TPU v7x, 32 devices: a whole 2x2x4 slice. The times are simulated.
32 devices in a mesh: groups: 1, cache: 16 (over z, y, x), dp: 2 (over core).
Axes of the slice: x: 2, y: 2, z: 4, core: 2. Of those that a mesh axis runs over, the one named last changes fastest.
Arguments:
- hidden: bfloat16 [640, 8192], P(('groups', 'dp'), 'cache'), may hold values from -6 to 6
- out_grad: bfloat16 [640, 8192], P(('groups', 'dp'), 'cache'), may hold values from -192 to 192
- norm_gain: float32 [8192], replicated, may hold values from 0.25 to 1.75
- w_query: bfloat16 [8192, 2048], P(None, 'cache'), may hold values from -0.0625 to 0.0625
- w_key: bfloat16 [8192, 8, 128], P(None, None, 'cache'), may hold values from -0.1875 to 0.1875
- w_value: bfloat16 [8192, 8, 128], P(None, None, 'cache'), may hold values from -0.0625 to 0.0625
- w_out: bfloat16 [2048, 8192], P('cache'), may hold values from -0.125 to 0.125
- cache_keys: float32 [1024, 1024], P(('groups', 'cache', 'dp')), may hold values from -512 to 512
- cache_values: float32 [1024, 1024], P(('groups', 'cache', 'dp')), may hold values from -6 to 6
- first_moment: float32 [2, 1024, 1024], P(None, ('groups', 'cache', 'dp')), may hold values from -0.1875 to 0.1875
- second_moment: float32 [2, 1024, 1024], P(None, ('groups', 'cache', 'dp')), may hold values from 0.0001 to 0.002
- conv_lengths: int32 [2, 4], P(('groups', 'dp')), may hold values from 1 to 160, 320 in all within a row
- row_offsets: int32 [2, 4], P(('groups', 'dp')), may hold values from 0 to 1023
Outputs:
- new_keys: float32 [1024, 1024], P(('groups', 'cache', 'dp'))
- new_values: float32 [1024, 1024], P(('groups', 'cache', 'dp'))
- new_first: float32 [2, 1024, 1024], P(None, ('groups', 'cache', 'dp'))
- new_second: float32 [2, 1024, 1024], P(None, ('groups', 'cache', 'dp'))
Inputs may be any that keep to these rules, and one draw needn't show every extreme that they name: `conv_lengths`: each dp index's 4 lengths sum to 320, and one of them is 160.
All inputs are finite; a program needn't handle non-finite values.
Results may differ from a plain program's by a relative error of at most 0.006.
The roundings to bfloat16 on the way count: a program that leaves them out, or rounds other values in their place, can miss the bound.
Values may be sent and summed in bfloat16 or wider, within the bound.
A program may use at most 128 MiB of HBM per device.

v0:
```python
import math
import jax
import jax.numpy as jnp
from jax import lax
from jax.sharding import PartitionSpec as P

KV = 8
ADAM_STEP = 10
THETA = 500000.0
BETA_ONE = 0.9
BETA_TWO = 0.999
RATE = 0.02
EPSILON = 1e-08


def rope_tables(position, head_width):
    half_width = head_width // 2
    inverse = jnp.exp(
        jnp.arange(half_width, dtype=jnp.float32) * (-2.0 * math.log(THETA) / head_width)
    )
    angles = position.astype(jnp.float32)[:, None] * inverse[None, :]
    return (jnp.cos(angles), jnp.sin(angles))


def rotate(tensor, cos_table, sin_table):
    half_width = tensor.shape[1] // 2
    first_half = tensor[:, :half_width]
    second_half = tensor[:, half_width:]
    return jnp.concatenate(
        [
            first_half * cos_table - second_half * sin_table,
            second_half * cos_table + first_half * sin_table,
        ],
        axis=1,
    )


def row_layout(lengths, offsets, row_count, cache_len):
    end_rows = jnp.cumsum(lengths)
    start_rows = end_rows - lengths
    row_index = jnp.arange(row_count, dtype=jnp.int32)
    segment = jnp.sum((row_index[:, None] >= end_rows[None, :]).astype(jnp.int32), axis=1)
    onehot = segment[:, None] == jnp.arange(lengths.shape[0], dtype=jnp.int32)[None, :]
    first_row = jnp.sum(jnp.where(onehot, start_rows[None, :], 0), axis=1)
    offset_row = jnp.sum(jnp.where(onehot, offsets[None, :], 0), axis=1)
    return (segment, cache_len + offset_row + row_index - first_row)


def attend(query, grad_out, cache_k, cache_v, self_k, self_v, allowed, score_scale):
    contract = (((1,), (1,)), ((), ()))
    score_cache = (
        lax.dot_general(query, cache_k, contract, preferred_element_type=jnp.float32) * score_scale
    )
    score_self = (
        lax.dot_general(query, self_k, contract, preferred_element_type=jnp.float32) * score_scale
    )
    score_self = jnp.where(allowed, score_self, -1e30)
    highest = jnp.maximum(
        jnp.max(score_cache, axis=1, keepdims=True), jnp.max(score_self, axis=1, keepdims=True)
    )
    exp_cache = jnp.exp(score_cache - highest)
    exp_self = jnp.exp(score_self - highest)
    denominator = jnp.sum(exp_cache, axis=1, keepdims=True) + jnp.sum(
        exp_self, axis=1, keepdims=True
    )
    prob_cache = exp_cache / denominator
    prob_self = exp_self / denominator
    weight_cache = prob_cache.astype(jnp.bfloat16)
    weight_self = prob_self.astype(jnp.bfloat16)
    attended = jnp.dot(weight_cache, cache_v, preferred_element_type=jnp.float32) + jnp.dot(
        weight_self, self_v, preferred_element_type=jnp.float32
    )
    delta_row = jnp.sum(grad_out.astype(jnp.float32) * attended, axis=1, keepdims=True)
    grad_prob = lax.dot_general(grad_out, cache_v, contract, preferred_element_type=jnp.float32)
    grad_score = (prob_cache * (grad_prob - delta_row)).astype(jnp.bfloat16)
    return (grad_score, weight_cache)


def adam_update(master, gradient, first, second):
    first_new = BETA_ONE * first + (1.0 - BETA_ONE) * gradient
    second_new = BETA_TWO * second + (1.0 - BETA_TWO) * gradient * gradient
    first_hat = first_new / (1.0 - BETA_ONE**ADAM_STEP)
    second_hat = second_new / (1.0 - BETA_TWO**ADAM_STEP)
    return (master - RATE * first_hat / (jnp.sqrt(second_hat) + EPSILON), first_new, second_new)


def source_total(pieces):
    head_width = pieces.shape[2]
    item_count = pieces.shape[1]
    summed = (
        pieces.astype(jnp.float32)
        .reshape(KV, pieces.shape[0] // KV, item_count, head_width)
        .sum(axis=1)
    )
    return summed.transpose(1, 0, 2).reshape(item_count, KV * head_width)


def totals_pair(pieces):
    return (source_total(pieces[0]), source_total(pieces[1]))


def per_device(
    hidden,
    out_grad,
    norm_gain,
    w_query,
    w_key,
    w_value,
    w_out,
    cache_keys,
    cache_values,
    first_moment,
    second_moment,
    conv_lengths,
    row_offsets,
):
    cache_count = lax.axis_size("cache")
    data_count = lax.axis_size("dp")
    pos_count = cache_keys.shape[0]
    device_count = cache_count * data_count
    cache_len = pos_count * device_count
    head_width = w_query.shape[1]
    column_share = w_key.shape[2]
    groups = cache_count // KV
    kv_head = lax.axis_index("cache") // groups
    score_scale = head_width ** (-0.5)
    hidden_full, grad_full = (
        lax.all_gather(hidden, "cache", axis=1, tiled=True),
        lax.all_gather(out_grad, "cache", axis=1, tiled=True),
    )
    row_count = hidden_full.shape[0]
    width_full = hidden_full.shape[1]
    hidden_f = hidden_full.astype(jnp.float32)
    inv_rms = lax.rsqrt(jnp.mean(hidden_f * hidden_f, axis=1, keepdims=True) + 1e-05)
    normed = (hidden_f * inv_rms * norm_gain).astype(jnp.bfloat16)
    segment, position = row_layout(conv_lengths[0], row_offsets[0], row_count, cache_len)
    cos_table, sin_table = rope_tables(position, head_width)
    query = rotate(
        jnp.dot(normed, w_query, preferred_element_type=jnp.float32), cos_table, sin_table
    ).astype(jnp.bfloat16)
    key_piece = (
        jnp.dot(
            normed, w_key.reshape(width_full, KV * column_share), preferred_element_type=jnp.float32
        )
        .astype(jnp.bfloat16)
        .reshape(row_count, KV, column_share)
    )
    value_piece = (
        jnp.dot(
            normed,
            w_value.reshape(width_full, KV * column_share),
            preferred_element_type=jnp.float32,
        )
        .astype(jnp.bfloat16)
        .reshape(row_count, KV, column_share)
    )
    keys_raw, values_self = (
        lax.all_gather(key_piece, "cache", axis=2, tiled=True),
        lax.all_gather(value_piece, "cache", axis=2, tiled=True),
    )
    own_keys = lax.dynamic_slice_in_dim(keys_raw, kv_head, 1, 1).reshape(row_count, head_width)
    self_k = rotate(own_keys.astype(jnp.float32), cos_table, sin_table).astype(jnp.bfloat16)
    self_v = lax.dynamic_slice_in_dim(values_self, kv_head, 1, 1).reshape(row_count, head_width)
    grad_out = lax.dot_general(
        grad_full, w_out, (((1,), (1,)), ((), ())), preferred_element_type=jnp.float32
    ).astype(jnp.bfloat16)
    cache_k = cache_keys.astype(jnp.bfloat16)
    cache_v = cache_values.astype(jnp.bfloat16)
    keys_all, values_all = (
        lax.all_gather(cache_k, ("cache", "dp"), axis=0, tiled=True),
        lax.all_gather(cache_v, ("cache", "dp"), axis=0, tiled=True),
    )
    head_k = lax.dynamic_slice_in_dim(keys_all, kv_head * head_width, head_width, 1)
    head_v = lax.dynamic_slice_in_dim(values_all, kv_head * head_width, head_width, 1)
    row_index = jnp.arange(row_count, dtype=jnp.int32)
    allowed = (segment[:, None] == segment[None, :]) & (row_index[None, :] <= row_index[:, None])
    grad_score, weight_cache = attend(
        query, grad_out, head_k, head_v, self_k, self_v, allowed, score_scale
    )
    transposed = (((0,), (0,)), ((), ()))
    key_part = (
        lax.dot_general(grad_score, query, transposed, preferred_element_type=jnp.float32)
        * score_scale
    ).astype(jnp.bfloat16)
    value_part = lax.dot_general(
        weight_cache, grad_out, transposed, preferred_element_type=jnp.float32
    ).astype(jnp.bfloat16)
    send_k = key_part.reshape(device_count, pos_count, head_width)
    send_v = value_part.reshape(device_count, pos_count, head_width)
    grad_k, grad_v = totals_pair(
        (
            lax.all_to_all(send_k, ("cache", "dp"), split_axis=0, concat_axis=0, tiled=True),
            lax.all_to_all(send_v, ("cache", "dp"), split_axis=0, concat_axis=0, tiled=True),
        )
    )
    gradient = jnp.stack([grad_k, grad_v])
    master = jnp.stack([cache_keys, cache_values])
    new_master, first_new, second_new = adam_update(master, gradient, first_moment, second_moment)
    return (new_master[0], new_master[1], first_new, second_new)


def solution(mesh):
    return jax.shard_map(
        per_device,
        mesh=mesh,
        in_specs=(
            P(("groups", "dp"), "cache"),
            P(("groups", "dp"), "cache"),
            P(),
            P(None, "cache"),
            P(None, None, "cache"),
            P(None, None, "cache"),
            P("cache", None),
            P(("groups", "cache", "dp"), None),
            P(("groups", "cache", "dp"), None),
            P(None, ("groups", "cache", "dp"), None),
            P(None, ("groups", "cache", "dp"), None),
            P(("groups", "dp"), None),
            P(("groups", "dp"), None),
        ),
        out_specs=(
            P(("groups", "cache", "dp"), None),
            P(("groups", "cache", "dp"), None),
            P(None, ("groups", "cache", "dp"), None),
            P(None, ("groups", "cache", "dp"), None),
        ),
        check_vma=False,
    )
```

profile of v0, /device:TPU:0, one launch (start us, length us, event | category | flops | bytes accessed | tf_op | source)
XLA Modules:
  0.0 358.8 jit_solution(13640633634136398060)
XLA Ops:
  7.2 0.7 all-gather.5.cloned.1.call-update
  8.0 1.5 convert_element_type.63
  9.6 0.7 all-gather.9.cloned.1.call-update
  10.3 1.5 convert_element_type.68
  11.9 0.8 reduce-window.4
  13.5 0.7 select_reduce_fusion.1
  14.3 90.2 %all-gather.5.cloned.1.call-done = bf16[320,8192]{1,0:T(8,128)(2,1)} async-done(((bf16[320,512]{1,0:T(8,128)(2,1)}), bf16[320,8192]{1,0:T(8,128)(2,1)}) %all-gather.5.cloned.1.call-update) | async-done | bytes 5242896 | tf_op jit(solution)/shard_map/all_gather | solution.py:128
  104.5 3.8 %fusion = f32[320]{0:T(512)S(1)} fusion(bf16[320,8192]{1,0:T(8,128)(2,1)} %all-gather.5.cloned.1.call-done), kind=kLoop, calls=%fused_computation.2 | loop fusion | flops 7864000 | bytes 5244160 | tf_op jit(solution)/shard_map/reduce_sum | solution.py:134
  108.5 1.6 fusion.2
  110.2 1.6 fusion.13
  111.8 0.7 copy-done.1
  112.5 43.7 %all_gather.20 = bf16[320,8,128]{0,1,2:T(8,128)(2,1)S(1)} all-gather(bf16[320,8,8]{0,1,2:T(8,128)(2,1)S(1)} %copy.24), channel_id=1, replica_groups=mesh['groups'=1,'cache'=16,'dp'=2] {'cache'}, dimensions={2}, use_global_device_ids=true | all-gather | bytes 696320 | tf_op jit(solution)/shard_map/all_gather | solution.py:158
  156.7 4.0 %fusion.59 = f32[320,128]{1,0:T(8,128)S(1)} fusion(bf16[320,8192]{1,0:T(8,128)(2,1)} %copy-done.1, bf16[8192,128]{1,0:T(8,128)(2,1)S(1)} %copy-done), kind=kOutput, calls=%fused_computation.93 | convolution fusion | flops 671088640 | bytes 7503872 | tf_op jit(solution)/shard_map/dot_general | solution.py:139
  160.7 0.7 fusion.41
  161.5 2.4 all-gather.7.cloned.1.call-done
  163.9 1.5 fusion.57
  166.3 4.1 %fusion.14 = bf16[320,8,8]{0,2,1:T(8,128)(2,1)S(1)} fusion(bf16[320,8192]{1,0:T(8,128)(2,1)} %copy-done.1, bf16[8192,8,8]{0,2,1:T(8,128)(2,1)S(1)} %copy-done.4), kind=kOutput, calls=%fused_computation.25 | convolution fusion | flops 335564800 | bytes 6332416 | tf_op jit(solution)/shard_map/dot_general | solution.py:149
  170.5 48.7 %all_gather.23 = bf16[320,8,128]{0,2,1:T(8,128)(2,1)S(1)} all-gather(bf16[320,8,8]{0,2,1:T(8,128)(2,1)S(1)} %fusion.14), channel_id=1, replica_groups=mesh['groups'=1,'cache'=16,'dp'=2] {'cache'}, dimensions={2}, use_global_device_ids=true | all-gather | bytes 696320 | tf_op jit(solution)/shard_map/all_gather | solution.py:159
  219.2 0.9 fusion.24
  220.4 40.8 %all-gather.9.cloned.1.call-done = bf16[320,8192]{1,0:T(8,128)(2,1)} async-done(((bf16[320,512]{1,0:T(8,128)(2,1)}), bf16[320,8192]{1,0:T(8,128)(2,1)}) %all-gather.9.cloned.1.call-update) | async-done | bytes 5242896 | tf_op jit(solution)/shard_map/all_gather | solution.py:129
  261.3 4.7 %convolution_convert_fusion.1 = bf16[320,128]{1,0:T(8,128)(2,1)S(1)} fusion(bf16[320,8192]{1,0:T(8,128)(2,1)} %all-gather.9.cloned.1.call-done, bf16[128,8192]{1,0:T(8,128)(2,1)} %param.19), kind=kOutput, calls=%fused_computation.20 | convolution fusion | flops 671129600 | bytes 7421952 | tf_op jit(solution)/shard_map/dot_general | solution.py:164
  265.9 53.2 %all-gather.11.cloned.1.call-done = bf16[1024,1024]{1,0:T(8,128)(2,1)} async-done(((bf16[32,1024]{1,0:T(8,128)(2,1)}), bf16[1024,1024]{1,0:T(8,128)(2,1)}) %all-gather.11.cloned.1.call-update) | async-done | bytes 2097168 | tf_op jit(solution)/shard_map/all_gather | solution.py:171
  319.1 1.4 fusion.12
  320.6 2.5 fusion.8
  323.0 3.6 all-to-all-start
  326.6 1.1 convolution_convert_fusion
  327.8 9.4 %all-to-all-done = bf16[32,32,128]{2,1,0:T(8,128)(2,1)} async-done(((bf16[32,32,128]{2,1,0:T(8,128)(2,1)}), bf16[32,32,128]{2,1,0:T(8,128)(2,1)}, u32[]{:S(2)}, u32[]{:S(2)}) %all-to-all-start) | async-done | bytes 262176 | tf_op jit(solution)/shard_map/all_to_all | solution.py:192
  337.2 2.6 all-to-all-start.1
  339.8 1.0 convert_reduce_fusion.1
  340.9 9.5 %all-to-all-done.1 = bf16[32,32,128]{2,1,0:T(8,128)(2,1)S(1)} async-done(((bf16[32,32,128]{2,1,0:T(8,128)(2,1)}), bf16[32,32,128]{2,1,0:T(8,128)(2,1)S(1)}, u32[]{:S(2)}, u32[]{:S(2)}) %all-to-all-start.1) | async-done | bytes 262176 | tf_op jit(solution)/shard_map/all_to_all | solution.py:193
  350.6 1.0 maximum_subtract_fusion
  351.6 0.7 slice_bitcast_fusion
  (51 shorter events, 3.1 us)
Async XLA Ops:
  7.2 149.5 %copy-start = (bf16[8192,128]{1,0:T(8,128)(2,1)S(1)}, bf16[8192,128]{1,0:T(8,128)(2,1)}, u32[]{:S(2)}) copy-start(bf16[8192,128]{1,0:T(8,128)(2,1)} %param.16) | copy-start | bytes 6291460
  7.2 97.3 %all-gather.5.cloned.1.call-start = ((), (), s32[]{:S(2)}) async-start(), calls=%async_computation.2 | async-start | bytes 5570560 | tf_op jit(solution)/shard_map/all_gather | solution.py:128
  7.9 156.0 %all-gather.7.cloned.1.call-start = ((), (), s32[]{:S(2)}) async-start(), calls=%async_computation.3 | async-start | bytes 2162688 | tf_op jit(solution)/shard_map/all_gather | solution.py:170
  9.5 251.7 %all-gather.9.cloned.1.call-start = ((), (), s32[]{:S(2)}) async-start(), calls=%async_computation.4 | async-start | bytes 5570560 | tf_op jit(solution)/shard_map/all_gather | solution.py:129
  10.3 308.9 %all-gather.11.cloned.1.call-start = ((), (), s32[]{:S(2)}) async-start(), calls=%async_computation.5 | async-start | bytes 2162688 | tf_op jit(solution)/shard_map/all_gather | solution.py:171
  11.9 96.4 %copy-start.11 = (f32[8192]{0:T(1024)S(1)}, f32[8192]{0:T(1024)}, u32[]{:S(2)}) copy-start(f32[8192]{0:T(1024)} %param.15) | copy-start | bytes 98308
  104.5 4.0 %copy-start.2 = (bf16[320,8192]{1,0:T(8,128)(2,1)S(1)}, bf16[320,8192]{1,0:T(8,128)(2,1)}, u32[]{:S(2)}) copy-start(bf16[320,8192]{1,0:T(8,128)(2,1)} %all-gather.5.cloned.1.call-done) | copy-start | bytes 15728644
  108.5 1.6 copy-start.3
  110.2 2.3 copy-start.1
  161.5 4.8 %copy-start.5 = (bf16[320,64]{1,0:T(8,128)(2,1)}, bf16[320,64]{1,0:T(8,128)(2,1)S(1)}, u32[]{:S(2)}) copy-start(bf16[320,64]{1,0:T(8,128)(2,1)S(1)} %get-tuple-element.15) | copy-start | bytes 122884
  161.5 4.8 %copy-start.6 = (bf16[320,64]{1,0:T(8,128)(2,1)}, bf16[320,64]{1,0:T(8,128)(2,1)S(1)}, u32[]{:S(2)}) copy-start(bf16[320,64]{1,0:T(8,128)(2,1)S(1)} %get-tuple-element.16) | copy-start | bytes 122884
  163.9 2.4 copy-start.4
  323.0 14.2 %all-to-all-start = ((bf16[32,32,128]{2,1,0:T(8,128)(2,1)}), bf16[32,32,128]{2,1,0:T(8,128)(2,1)}, u32[]{:S(2)}, u32[]{:S(2)}) async-start(bf16[32,32,128]{2,1,0:T(8,128)(2,1)} %bitcast.50), calls=%async_computation | async-start | bytes 524288 | tf_op jit(solution)/shard_map/all_to_all | solution.py:192
  327.7 22.8 %copy-start.7 = (f32[32,1024]{1,0:T(8,128)S(1)}, f32[32,1024]{1,0:T(8,128)}, u32[]{:S(2)}) copy-start(f32[32,1024]{1,0:T(8,128)} %param.21) | copy-start | bytes 393220
  327.7 22.8 %copy-start.8 = (f32[32,1024]{1,0:T(8,128)S(1)}, f32[32,1024]{1,0:T(8,128)}, u32[]{:S(2)}) copy-start(f32[32,1024]{1,0:T(8,128)} %param.20) | copy-start | bytes 393220
  327.7 22.8 %copy-start.9 = (f32[2,32,1024]{2,1,0:T(8,128)S(1)}, f32[2,32,1024]{2,1,0:T(8,128)}, u32[]{:S(2)}) copy-start(f32[2,32,1024]{2,1,0:T(8,128)} %param.22) | copy-start | bytes 786436
  327.7 22.9 %copy-start.10 = (f32[2,32,1024]{2,1,0:T(8,128)S(1)}, f32[2,32,1024]{2,1,0:T(8,128)}, u32[]{:S(2)}) copy-start(f32[2,32,1024]{2,1,0:T(8,128)} %param.23) | copy-start | bytes 786436
  337.2 13.2 %all-to-all-start.1 = ((bf16[32,32,128]{2,1,0:T(8,128)(2,1)}), bf16[32,32,128]{2,1,0:T(8,128)(2,1)S(1)}, u32[]{:S(2)}, u32[]{:S(2)}) async-start(bf16[32,32,128]{2,1,0:T(8,128)(2,1)} %bitcast.49), calls=%async_computation.1 | async-start | bytes 524288 | tf_op jit(solution)/shard_map/all_to_all | solution.py:193
Sparse Core Ops, SparseCore 0:
  10.7 93.6 all-gather.4
  107.9 55.9 all-gather.6
  166.7 94.5 all-gather.8
  264.6 54.5 all-gather.10
where the time goes:
time: 359 us
  waiting for transfers between devices  207 us (58%)
  blocking collectives  92.5 us (26%)
  matrix products  22.3 us (6%)
  other arithmetic  14.4 us (4%)
  between operations  14.1 us (4%)
  starting transfers between devices  6.33 us (2%)
    all_gather x1, waiting for transfers between devices, per_device(): lax.all_gather(hidden, 'cache', axis=1, tiled=True)  90.2 us
    all_gather x1, waiting for transfers between devices, per_device(): lax.all_gather(cache_v, ('cache', 'dp'), axis=0, tiled=True)  53.2 us
    all_gather x1, blocking collectives, per_device(): lax.all_gather(value_piece, 'cache', axis=2, tiled=True)  48.7 us
    all_gather x1, blocking collectives, per_device(): lax.all_gather(key_piece, 'cache', axis=2, tiled=True)  43.7 us
    all_gather x1, waiting for transfers between devices, per_device(): lax.all_gather(out_grad, 'cache', axis=1, tiled=True)  40.8 us
    all_to_all x1, waiting for transfers between devices, per_device(): lax.all_to_all(send_v, ('cache', 'dp'), split_axis=0, concat_axis=0, tile...  9.46 us
    all_to_all x1, waiting for transfers between devices, per_device(): lax.all_to_all(send_k, ('cache', 'dp'), split_axis=0, concat_axis=0, tile...  9.45 us
  transfers between devices with their start and end apart: 6, of which 6 were waited for; matrix products, arithmetic and copies ran while one was open for 9% of the time, Pallas kernels for 0%

commit v1 on v0

--- a/solution.py
+++ b/solution.py
@@ -11,6 +11,24 @@
 BETA_TWO = 0.999
 RATE = 0.02
 EPSILON = 1e-08
+
+
+def ring_gather(array, axis, dim):
+    ways, here, lap = (lax.axis_size(axis), lax.axis_index(axis), array.shape[dim])
+    dims = [n * ways if d == dim else n for d, n in enumerate(array.shape)]
+    full = lax.dynamic_update_slice_in_dim(
+        jnp.zeros(dims, array.dtype), array, here * lap, axis=dim
+    )
+    going_up = going_down = array
+    for far in range(1, ways // 2 + 1):
+        going_up = lax.ppermute(going_up, axis, [(d, (d + 1) % ways) for d in range(ways)])
+        full = lax.dynamic_update_slice_in_dim(full, going_up, (here - far) % ways * lap, axis=dim)
+        if 2 * far < ways:
+            going_down = lax.ppermute(going_down, axis, [(d, (d - 1) % ways) for d in range(ways)])
+            full = lax.dynamic_update_slice_in_dim(
+                full, going_down, (here + far) % ways * lap, axis=dim
+            )
+    return full
 
 
 def rope_tables(position, head_width):
@@ -156,7 +174,7 @@
     )
     keys_raw, values_self = (
         lax.all_gather(key_piece, "cache", axis=2, tiled=True),
-        lax.all_gather(value_piece, "cache", axis=2, tiled=True),
+        ring_gather(value_piece, "cache", 2),
     )
     own_keys = lax.dynamic_slice_in_dim(keys_raw, kv_head, 1, 1).reshape(row_count, head_width)
     self_k = rotate(own_keys.astype(jnp.float32), cos_table, sin_table).astype(jnp.bfloat16)

time: 359 us -> 398 us (1.11)
  blocking collectives: 92.5 us -> 43.2 us
  starting transfers between devices: 6.33 us -> 46.2 us
  waiting for transfers between devices: 207 us -> 246 us
  local copies, waits for them, and re-layouts: 2.34 us -> 13.6 us
    all_gather x1 -> x0, blocking collectives: 48.7 us -> none  [per_device(): lax.all_gather(value_piece, 'cache', axis=2, tiled=True)]
    all_gather x1, waiting for transfers between devices: 40.8 us -> 85.9 us  [per_device(): lax.all_gather(out_grad, 'cache', axis=1, tiled=True)]
    ppermute x0 -> x15, starting transfers between devices: none -> 39.8 us  [the longest x7 36.8 us: ring_gather(): lax.ppermute(going_down, axis, [(d, (d - 1) % ways) for d in range(ways)])]
    dynamic_update_slice x0 -> x15, local copies, waits for them, and re-layouts: none -> 11 us  [the longest x8 5.83 us: ring_gather(): lax.dynamic_update_slice_in_dim(full, going_up, (here - far) % ways * lap...]
    ppermute x0 -> x15, waiting for transfers between devices: none -> 10.2 us  [the longest x8 10.2 us: ring_gather(): lax.ppermute(going_up, axis, [(d, (d + 1) % ways) for d in range(ways)])]
    all_to_all x1, waiting for transfers between devices: 9.46 us -> 0.01 us  [per_device(): lax.all_to_all(send_v, ('cache', 'dp'), split_axis=0, concat_axis=0, tile...]
    all_gather x1, waiting for transfers between devices: 53.2 us -> 48.8 us  [per_device(): lax.all_gather(cache_v, ('cache', 'dp'), axis=0, tiled=True)]
  transfers between devices with their start and end apart: 6 -> 21, of which waited for: 6 -> 10; matrix products, arithmetic and copies ran while one was open for 9% -> 11% of each run, Pallas kernels for 0% -> 0%
where the time goes in v1:
time: 398 us; the launch traced here: 397 us
  waiting for transfers between devices  246 us (62%)
  starting transfers between devices  46.2 us (12%)
  blocking collectives  43.2 us (11%)
  matrix products  20 us (5%)
  between operations  14.5 us (4%)
  other arithmetic  14.4 us (4%)
  local copies, waits for them, and re-layouts  13.6 us (3%)
    all_gather x1, waiting for transfers between devices, per_device(): lax.all_gather(hidden, 'cache', axis=1, tiled=True)  89.9 us
    all_gather x1, waiting for transfers between devices, per_device(): lax.all_gather(out_grad, 'cache', axis=1, tiled=True)  85.9 us
    all_gather x1, waiting for transfers between devices, per_device(): lax.all_gather(cache_v, ('cache', 'dp'), axis=0, tiled=True)  48.8 us
    all_gather x1, blocking collectives, per_device(): lax.all_gather(key_piece, 'cache', axis=2, tiled=True)  43.2 us
    ppermute x7, starting transfers between devices, ring_gather(): lax.ppermute(going_down, axis, [(d, (d - 1) % ways) for d in range(ways)])  36.8 us
    ppermute x8, waiting for transfers between devices, ring_gather(): lax.ppermute(going_up, axis, [(d, (d + 1) % ways) for d in range(ways)])  10.2 us
    all_to_all x1, waiting for transfers between devices, per_device(): lax.all_to_all(send_k, ('cache', 'dp'), split_axis=0, concat_axis=0, tile...  9.47 us
  transfers between devices with their start and end apart: 21, of which 10 were waited for; matrix products, arithmetic and copies ran while one was open for 11% of the time, Pallas kernels for 0%

profile of v1, /device:TPU:0, one launch (start us, length us, event | category | flops | bytes accessed | tf_op | source)
XLA Modules:
  0.0 397.4 jit_solution(6505183119209014575)
XLA Ops:
  8.0 1.5 convert_element_type.63
  10.3 1.5 convert_element_type.68
  14.6 89.9 %all-gather.5.cloned.1.call-done = bf16[320,8192]{1,0:T(8,128)(2,1)} async-done(((bf16[320,512]{1,0:T(8,128)(2,1)}), bf16[320,8192]{1,0:T(8,128)(2,1)}) %all-gather.5.cloned.1.call-update) | async-done | bytes 5242896 | tf_op jit(solution)/shard_map/all_gather | solution.py:146
  104.5 3.8 fusion
  108.5 1.6 fusion.2
  110.3 1.7 constant_dynamic-update-slice_fusion.17
  111.9 1.5 collective-permute-start
  113.4 4.2 %collective-permute-start.1 = (bf16[320,8,8]{0,2,1:T(8,128)(2,1)S(1)}, bf16[320,8,8]{0,2,1:T(8,128)(2,1)}, u32[]{:S(2)}, u32[]{:S(2)}) collective-permute-start(bf16[320,8,8]{0,2,1:T(8,128)(2,1)S(1)} %get-tuple-element.22), channel_id=1, source_target_pairs={{0,30},{2,0},{4,2},{6,4},{8,6},{10,8},{12,10},{14,12},{16,14},{18,... | collective-permute-start | bytes 122888 | tf_op jit(solution)/shard_map/ppermute | solution.py:27
  117.6 1.6 fusion.13
  119.3 43.2 %all_gather.17 = bf16[320,8,128]{0,1,2:T(8,128)(2,1)S(1)} all-gather(bf16[320,8,8]{0,1,2:T(8,128)(2,1)S(1)} %copy.24), channel_id=1, replica_groups=mesh['groups'=1,'cache'=16,'dp'=2] {'cache'}, dimensions={2}, use_global_device_ids=true | all-gather | bytes 696320 | tf_op jit(solution)/shard_map/all_gather | solution.py:176
  162.9 4.0 %fusion.59 = f32[320,128]{1,0:T(8,128)S(1)} fusion(bf16[320,8192]{1,0:T(8,128)(2,1)} %copy-done.1, bf16[8192,128]{1,0:T(8,128)(2,1)S(1)} %copy-done), kind=kOutput, calls=%fused_computation.109 | convolution fusion | flops 671088640 | bytes 7503872 | tf_op jit(solution)/shard_map/dot_general | solution.py:157
  167.7 1.4 fusion.57
  171.1 85.9 %all-gather.9.cloned.1.call-done = bf16[320,8192]{1,0:T(8,128)(2,1)} async-done(((bf16[320,512]{1,0:T(8,128)(2,1)}), bf16[320,8192]{1,0:T(8,128)(2,1)}) %all-gather.9.cloned.1.call-update) | async-done | bytes 5242896 | tf_op jit(solution)/shard_map/all_gather | solution.py:147
  257.1 4.7 %convolution_convert_fusion.1 = bf16[320,128]{1,0:T(8,128)(2,1)S(1)} fusion(bf16[320,8192]{1,0:T(8,128)(2,1)} %all-gather.9.cloned.1.call-done, bf16[128,8192]{1,0:T(8,128)(2,1)} %param.19), kind=kOutput, calls=%fused_computation.20 | convolution fusion | flops 671129600 | bytes 7421952 | tf_op jit(solution)/shard_map/dot_general | solution.py:182
  261.7 1.1 convolution_convert_fusion
  262.8 3.5 all-to-all-start.1
  266.3 48.8 %all-gather.11.cloned.1.call-done = bf16[1024,1024]{1,0:T(8,128)(2,1)} async-done(((bf16[32,1024]{1,0:T(8,128)(2,1)}), bf16[1024,1024]{1,0:T(8,128)(2,1)}) %all-gather.11.cloned.1.call-update) | async-done | bytes 2097168 | tf_op jit(solution)/shard_map/all_gather | solution.py:189
  315.2 1.3 fusion.21
  316.5 1.5 collective-permute-start.2
  318.0 4.2 %collective-permute-start.3 = (bf16[320,8,8]{0,2,1:T(8,128)(2,1)}, bf16[320,8,8]{0,2,1:T(8,128)(2,1)S(1)}, u32[]{:S(2)}, u32[]{:S(2)}) collective-permute-start(bf16[320,8,8]{0,2,1:T(8,128)(2,1)} %collective-permute-done.1), channel_id=1, source_target_pairs={{0,30},{2,0},{4,2},{6,4},{8,6},{10,8},{12,10},{14,12},{16,14},{18,... | collective-permute-start | bytes 122888 | tf_op jit(solution)/shard_map/ppermute | solution.py:27
  322.2 1.4 constant_dynamic-update-slice_fusion.16
  323.6 1.4 constant_dynamic-update-slice_fusion.15
  325.1 5.6 %collective-permute-start.5 = (bf16[320,8,8]{0,2,1:T(8,128)(2,1)S(1)}, bf16[320,8,8]{0,2,1:T(8,128)(2,1)S(1)}, u32[]{:S(2)}, u32[]{:S(2)}) collective-permute-start(bf16[320,8,8]{0,2,1:T(8,128)(2,1)S(1)} %collective-permute-done.3), channel_id=1, source_target_pairs={{0,30},{2,0},{4,2},{6,4},{8,6},{10,8},{12,10},{14,12},{16,14},{18,... | collective-permute-start | bytes 122888 | tf_op jit(solution)/shard_map/ppermute | solution.py:27
  332.8 5.7 %collective-permute-start.7 = (bf16[320,8,8]{0,2,1:T(8,128)(2,1)S(1)}, bf16[320,8,8]{0,2,1:T(8,128)(2,1)S(1)}, u32[]{:S(2)}, u32[]{:S(2)}) collective-permute-start(bf16[320,8,8]{0,2,1:T(8,128)(2,1)S(1)} %collective-permute-done.5), channel_id=1, source_target_pairs={{0,30},{2,0},{4,2},{6,4},{8,6},{10,8},{12,10},{14,12},{16,14},{18,... | collective-permute-start | bytes 122888 | tf_op jit(solution)/shard_map/ppermute | solution.py:27
  340.5 5.6 %collective-permute-start.9 = (bf16[320,8,8]{0,2,1:T(8,128)(2,1)S(1)}, bf16[320,8,8]{0,2,1:T(8,128)(2,1)S(1)}, u32[]{:S(2)}, u32[]{:S(2)}) collective-permute-start(bf16[320,8,8]{0,2,1:T(8,128)(2,1)S(1)} %collective-permute-done.7), channel_id=1, source_target_pairs={{0,30},{2,0},{4,2},{6,4},{8,6},{10,8},{12,10},{14,12},{16,14},{18,... | collective-permute-start | bytes 122888 | tf_op jit(solution)/shard_map/ppermute | solution.py:27
  348.2 5.7 %collective-permute-start.11 = (bf16[320,8,8]{0,2,1:T(8,128)(2,1)S(1)}, bf16[320,8,8]{0,2,1:T(8,128)(2,1)S(1)}, u32[]{:S(2)}, u32[]{:S(2)}) collective-permute-start(bf16[320,8,8]{0,2,1:T(8,128)(2,1)S(1)} %collective-permute-done.9), channel_id=1, source_target_pairs={{0,30},{2,0},{4,2},{6,4},{8,6},{10,8},{12,10},{14,12},{16,14},{18,... | collective-permute-start | bytes 122888 | tf_op jit(solution)/shard_map/ppermute | solution.py:27
  355.9 5.7 %collective-permute-start.13 = (bf16[320,8,8]{0,2,1:T(8,128)(2,1)S(1)}, bf16[320,8,8]{0,2,1:T(8,128)(2,1)S(1)}, u32[]{:S(2)}, u32[]{:S(2)}) collective-permute-start(bf16[320,8,8]{0,2,1:T(8,128)(2,1)S(1)} %collective-permute-done.11), channel_id=1, source_target_pairs={{0,30},{2,0},{4,2},{6,4},{8,6},{10,8},{12,10},{14,12},{16,14},{18,... | collective-permute-start | bytes 122888 | tf_op jit(solution)/shard_map/ppermute | solution.py:27
  364.9 6.4 %collective-permute-done.14 = bf16[320,8,8]{0,2,1:T(8,128)(2,1)S(1)} collective-permute-done((bf16[320,8,8]{0,2,1:T(8,128)(2,1)S(1)}, bf16[320,8,8]{0,2,1:T(8,128)(2,1)S(1)}, u32[]{:S(2)}, u32[]{:S(2)}) %collective-permute-start.14) | collective-permute-done | bytes 40992 | tf_op jit(solution)/shard_map/ppermute | solution.py:24
  371.9 1.3 fusion.12
  373.2 2.5 fusion.8
  375.7 2.7 all-to-all-start
  379.5 9.5 %all-to-all-done = bf16[32,32,128]{2,1,0:T(8,128)(2,1)S(1)} async-done(((bf16[32,32,128]{2,1,0:T(8,128)(2,1)}), bf16[32,32,128]{2,1,0:T(8,128)(2,1)S(1)}, u32[]{:S(2)}, u32[]{:S(2)}) %all-to-all-start) | async-done | bytes 262176 | tf_op jit(solution)/shard_map/all_to_all | solution.py:210
  (102 shorter events, 22.4 us)
Async XLA Ops:
  7.2 155.7 %copy-start = (bf16[8192,128]{1,0:T(8,128)(2,1)S(1)}, bf16[8192,128]{1,0:T(8,128)(2,1)}, u32[]{:S(2)}) copy-start(bf16[8192,128]{1,0:T(8,128)(2,1)} %param.16) | copy-start | bytes 6291460
  7.2 97.3 %all-gather.5.cloned.1.call-start = ((), (), s32[]{:S(2)}) async-start(), calls=%async_computation.2 | async-start | bytes 5570560 | tf_op jit(solution)/shard_map/all_gather | solution.py:146
  7.9 159.8 %all-gather.7.cloned.1.call-start = ((), (), s32[]{:S(2)}) async-start(), calls=%async_computation.3 | async-start | bytes 2162688 | tf_op jit(solution)/shard_map/all_gather | solution.py:188
  9.5 247.5 %all-gather.9.cloned.1.call-start = ((), (), s32[]{:S(2)}) async-start(), calls=%async_computation.4 | async-start | bytes 5570560 | tf_op jit(solution)/shard_map/all_gather | solution.py:147
  10.3 304.9 %all-gather.11.cloned.1.call-start = ((), (), s32[]{:S(2)}) async-start(), calls=%async_computation.5 | async-start | bytes 2162688 | tf_op jit(solution)/shard_map/all_gather | solution.py:189
  12.2 96.1 %copy-start.14 = (f32[8192]{0:T(1024)S(1)}, f32[8192]{0:T(1024)}, u32[]{:S(2)}) copy-start(f32[8192]{0:T(1024)} %param.15) | copy-start | bytes 98308
  104.5 4.0 %copy-start.2 = (bf16[320,8192]{1,0:T(8,128)(2,1)S(1)}, bf16[320,8192]{1,0:T(8,128)(2,1)}, u32[]{:S(2)}) copy-start(bf16[320,8192]{1,0:T(8,128)(2,1)} %all-gather.5.cloned.1.call-done) | copy-start | bytes 15728644
  110.1 7.5 %copy-start.1 = (bf16[320,8192]{1,0:T(8,128)(2,1)}, bf16[320,8192]{1,0:T(8,128)(2,1)S(1)}, u32[]{:S(2)}) copy-start(bf16[320,8192]{1,0:T(8,128)(2,1)S(1)} %fusion.2) | copy-start | bytes 15728644
  110.2 7.4 %copy-start.3 = (bf16[8192,8,8]{0,2,1:T(8,128)(2,1)S(1)}, bf16[8192,8,8]{0,2,1:T(8,128)(2,1)}, u32[]{:S(2)}) copy-start(bf16[8192,8,8]{0,2,1:T(8,128)(2,1)} %param.17) | copy-start | bytes 3145732
  111.9 7.3 %copy-start.5 = (bf16[320,8,128]{0,2,1:T(8,128)(2,1)}, bf16[320,8,128]{0,2,1:T(8,128)(2,1)S(1)}, u32[]{:S(2)}) copy-start(bf16[320,8,128]{0,2,1:T(8,128)(2,1)S(1)} %get-tuple-element.21) | copy-start | bytes 1966084
  111.9 204.6 %collective-permute-start = (bf16[320,8,8]{0,2,1:T(8,128)(2,1)S(1)}, bf16[320,8,8]{0,2,1:T(8,128)(2,1)}, u32[]{:S(2)}, u32[]{:S(2)}) collective-permute-start(bf16[320,8,8]{0,2,1:T(8,128)(2,1)S(1)} %get-tuple-element.22), channel_id=1, source_target_pairs={{0,2},{2,4},{4,6},{6,8},{8,10},{10,12},{12,14},{14,16},{16,18},{18... | collective-permute-start | bytes 122888 | tf_op jit(solution)/shard_map/ppermute | solution.py:24
  113.4 204.6 %collective-permute-start.1 = (bf16[320,8,8]{0,2,1:T(8,128)(2,1)S(1)}, bf16[320,8,8]{0,2,1:T(8,128)(2,1)}, u32[]{:S(2)}, u32[]{:S(2)}) collective-permute-start(bf16[320,8,8]{0,2,1:T(8,128)(2,1)S(1)} %get-tuple-element.22), channel_id=1, source_target_pairs={{0,30},{2,0},{4,2},{6,4},{8,6},{10,8},{12,10},{14,12},{16,14},{18,... | collective-permute-start | bytes 122888 | tf_op jit(solution)/shard_map/ppermute | solution.py:27
  262.8 112.8 %all-to-all-start.1 = ((bf16[32,32,128]{2,1,0:T(8,128)(2,1)}), bf16[32,32,128]{2,1,0:T(8,128)(2,1)}, u32[]{:S(2)}, u32[]{:S(2)}) async-start(bf16[32,32,128]{2,1,0:T(8,128)(2,1)} %bitcast.51), calls=%async_computation.1 | async-start | bytes 524288 | tf_op jit(solution)/shard_map/all_to_all | solution.py:211
  315.2 56.8 %copy-start.11 = (f32[320,320]{0,1:T(8,128)S(1)}, f32[320,320]{0,1:T(8,128)}, u32[]{:S(2)}) copy-start(f32[320,320]{0,1:T(8,128)} %copy-done.10) | copy-start | bytes 1228804
  316.5 8.5 %collective-permute-start.2 = (bf16[320,8,8]{0,2,1:T(8,128)(2,1)}, bf16[320,8,8]{0,2,1:T(8,128)(2,1)S(1)}, u32[]{:S(2)}, u32[]{:S(2)}) collective-permute-start(bf16[320,8,8]{0,2,1:T(8,128)(2,1)} %collective-permute-done), channel_id=1, source_target_pairs={{0,2},{2,4},{4,6},{6,8},{8,10},{10,12},{12,14},{14,16},{16,18},{18... | collective-permute-start | bytes 122888 | tf_op jit(solution)/shard_map/ppermute | solution.py:24
  318.0 7.1 %collective-permute-start.3 = (bf16[320,8,8]{0,2,1:T(8,128)(2,1)}, bf16[320,8,8]{0,2,1:T(8,128)(2,1)S(1)}, u32[]{:S(2)}, u32[]{:S(2)}) collective-permute-start(bf16[320,8,8]{0,2,1:T(8,128)(2,1)} %collective-permute-done.1), channel_id=1, source_target_pairs={{0,30},{2,0},{4,2},{6,4},{8,6},{10,8},{12,10},{14,12},{16,14},{18,... | collective-permute-start | bytes 122888 | tf_op jit(solution)/shard_map/ppermute | solution.py:27
  325.1 7.7 %collective-permute-start.4 = (bf16[320,8,8]{0,2,1:T(8,128)(2,1)S(1)}, bf16[320,8,8]{0,2,1:T(8,128)(2,1)S(1)}, u32[]{:S(2)}, u32[]{:S(2)}) collective-permute-start(bf16[320,8,8]{0,2,1:T(8,128)(2,1)S(1)} %collective-permute-done.2), channel_id=1, source_target_pairs={{0,2},{2,4},{4,6},{6,8},{8,10},{10,12},{12,14},{14,16},{16,18},{18... | collective-permute-start | bytes 122888 | tf_op jit(solution)/shard_map/ppermute | solution.py:24
  325.1 7.7 %collective-permute-start.5 = (bf16[320,8,8]{0,2,1:T(8,128)(2,1)S(1)}, bf16[320,8,8]{0,2,1:T(8,128)(2,1)S(1)}, u32[]{:S(2)}, u32[]{:S(2)}) collective-permute-start(bf16[320,8,8]{0,2,1:T(8,128)(2,1)S(1)} %collective-permute-done.3), channel_id=1, source_target_pairs={{0,30},{2,0},{4,2},{6,4},{8,6},{10,8},{12,10},{14,12},{16,14},{18,... | collective-permute-start | bytes 122888 | tf_op jit(solution)/shard_map/ppermute | solution.py:27
  332.7 7.8 %collective-permute-start.6 = (bf16[320,8,8]{0,2,1:T(8,128)(2,1)S(1)}, bf16[320,8,8]{0,2,1:T(8,128)(2,1)S(1)}, u32[]{:S(2)}, u32[]{:S(2)}) collective-permute-start(bf16[320,8,8]{0,2,1:T(8,128)(2,1)S(1)} %collective-permute-done.4), channel_id=1, source_target_pairs={{0,2},{2,4},{4,6},{6,8},{8,10},{10,12},{12,14},{14,16},{16,18},{18... | collective-permute-start | bytes 122888 | tf_op jit(solution)/shard_map/ppermute | solution.py:24
  332.8 7.8 %collective-permute-start.7 = (bf16[320,8,8]{0,2,1:T(8,128)(2,1)S(1)}, bf16[320,8,8]{0,2,1:T(8,128)(2,1)S(1)}, u32[]{:S(2)}, u32[]{:S(2)}) collective-permute-start(bf16[320,8,8]{0,2,1:T(8,128)(2,1)S(1)} %collective-permute-done.5), channel_id=1, source_target_pairs={{0,30},{2,0},{4,2},{6,4},{8,6},{10,8},{12,10},{14,12},{16,14},{18,... | collective-permute-start | bytes 122888 | tf_op jit(solution)/shard_map/ppermute | solution.py:27
  340.5 7.7 %collective-permute-start.8 = (bf16[320,8,8]{0,2,1:T(8,128)(2,1)S(1)}, bf16[320,8,8]{0,2,1:T(8,128)(2,1)S(1)}, u32[]{:S(2)}, u32[]{:S(2)}) collective-permute-start(bf16[320,8,8]{0,2,1:T(8,128)(2,1)S(1)} %collective-permute-done.6), channel_id=1, source_target_pairs={{0,2},{2,4},{4,6},{6,8},{8,10},{10,12},{12,14},{14,16},{16,18},{18... | collective-permute-start | bytes 122888 | tf_op jit(solution)/shard_map/ppermute | solution.py:24
  340.5 7.7 %collective-permute-start.9 = (bf16[320,8,8]{0,2,1:T(8,128)(2,1)S(1)}, bf16[320,8,8]{0,2,1:T(8,128)(2,1)S(1)}, u32[]{:S(2)}, u32[]{:S(2)}) collective-permute-start(bf16[320,8,8]{0,2,1:T(8,128)(2,1)S(1)} %collective-permute-done.7), channel_id=1, source_target_pairs={{0,30},{2,0},{4,2},{6,4},{8,6},{10,8},{12,10},{14,12},{16,14},{18,... | collective-permute-start | bytes 122888 | tf_op jit(solution)/shard_map/ppermute | solution.py:27
  348.2 7.7 %collective-permute-start.10 = (bf16[320,8,8]{0,2,1:T(8,128)(2,1)S(1)}, bf16[320,8,8]{0,2,1:T(8,128)(2,1)S(1)}, u32[]{:S(2)}, u32[]{:S(2)}) collective-permute-start(bf16[320,8,8]{0,2,1:T(8,128)(2,1)S(1)} %collective-permute-done.8), channel_id=1, source_target_pairs={{0,2},{2,4},{4,6},{6,8},{8,10},{10,12},{12,14},{14,16},{16,18},{18... | collective-permute-start | bytes 122888 | tf_op jit(solution)/shard_map/ppermute | solution.py:24
  348.2 7.7 %collective-permute-start.11 = (bf16[320,8,8]{0,2,1:T(8,128)(2,1)S(1)}, bf16[320,8,8]{0,2,1:T(8,128)(2,1)S(1)}, u32[]{:S(2)}, u32[]{:S(2)}) collective-permute-start(bf16[320,8,8]{0,2,1:T(8,128)(2,1)S(1)} %collective-permute-done.9), channel_id=1, source_target_pairs={{0,30},{2,0},{4,2},{6,4},{8,6},{10,8},{12,10},{14,12},{16,14},{18,... | collective-permute-start | bytes 122888 | tf_op jit(solution)/shard_map/ppermute | solution.py:27
  355.9 7.7 %collective-permute-start.12 = (bf16[320,8,8]{0,2,1:T(8,128)(2,1)S(1)}, bf16[320,8,8]{0,2,1:T(8,128)(2,1)S(1)}, u32[]{:S(2)}, u32[]{:S(2)}) collective-permute-start(bf16[320,8,8]{0,2,1:T(8,128)(2,1)S(1)} %collective-permute-done.10), channel_id=1, source_target_pairs={{0,2},{2,4},{4,6},{6,8},{8,10},{10,12},{12,14},{14,16},{16,18},{18... | collective-permute-start | bytes 122888 | tf_op jit(solution)/shard_map/ppermute | solution.py:24
  355.9 8.3 %collective-permute-start.13 = (bf16[320,8,8]{0,2,1:T(8,128)(2,1)S(1)}, bf16[320,8,8]{0,2,1:T(8,128)(2,1)S(1)}, u32[]{:S(2)}, u32[]{:S(2)}) collective-permute-start(bf16[320,8,8]{0,2,1:T(8,128)(2,1)S(1)} %collective-permute-done.11), channel_id=1, source_target_pairs={{0,30},{2,0},{4,2},{6,4},{8,6},{10,8},{12,10},{14,12},{16,14},{18,... | collective-permute-start | bytes 122888 | tf_op jit(solution)/shard_map/ppermute | solution.py:27
  363.6 7.7 %collective-permute-start.14 = (bf16[320,8,8]{0,2,1:T(8,128)(2,1)S(1)}, bf16[320,8,8]{0,2,1:T(8,128)(2,1)S(1)}, u32[]{:S(2)}, u32[]{:S(2)}) collective-permute-start(bf16[320,8,8]{0,2,1:T(8,128)(2,1)S(1)} %collective-permute-done.12), channel_id=1, source_target_pairs={{0,2},{2,4},{4,6},{6,8},{8,10},{10,12},{12,14},{14,16},{16,18},{18... | collective-permute-start | bytes 122888 | tf_op jit(solution)/shard_map/ppermute | solution.py:24
  375.6 13.6 %copy-start.8 = (f32[32,1024]{1,0:T(8,128)S(1)}, f32[32,1024]{1,0:T(8,128)}, u32[]{:S(2)}) copy-start(f32[32,1024]{1,0:T(8,128)} %param.21) | copy-start | bytes 393220
  375.6 13.6 %copy-start.9 = (f32[32,1024]{1,0:T(8,128)S(1)}, f32[32,1024]{1,0:T(8,128)}, u32[]{:S(2)}) copy-start(f32[32,1024]{1,0:T(8,128)} %param.20) | copy-start | bytes 393220
  375.6 13.6 %copy-start.12 = (f32[2,32,1024]{2,1,0:T(8,128)S(1)}, f32[2,32,1024]{2,1,0:T(8,128)}, u32[]{:S(2)}) copy-start(f32[2,32,1024]{2,1,0:T(8,128)} %param.22) | copy-start | bytes 786436
  375.6 13.6 %copy-start.13 = (f32[2,32,1024]{2,1,0:T(8,128)S(1)}, f32[2,32,1024]{2,1,0:T(8,128)}, u32[]{:S(2)}) copy-start(f32[2,32,1024]{2,1,0:T(8,128)} %param.23) | copy-start | bytes 786436
  375.7 13.3 %all-to-all-start = ((bf16[32,32,128]{2,1,0:T(8,128)(2,1)}), bf16[32,32,128]{2,1,0:T(8,128)(2,1)S(1)}, u32[]{:S(2)}, u32[]{:S(2)}) async-start(bf16[32,32,128]{2,1,0:T(8,128)(2,1)} %bitcast.52), calls=%async_computation | async-start | bytes 524288 | tf_op jit(solution)/shard_map/all_to_all | solution.py:210
  (4 other events, 8.8 us)
Sparse Core Ops, SparseCore 0:
  10.7 93.6 all-gather.4
  107.9 56.6 all-gather.6
  167.4 89.6 all-gather.8
  259.8 55.3 all-gather.10
